TPU v7x, 32 devices: a whole 2x2x4 slice. The times are simulated.
32 devices in a mesh: section: 4 (over z), tm: 4 (over y, x), batch: 2 (over core).
Axes of the slice: x: 2, y: 2, z: 4, core: 2. Of those that a mesh axis runs over, the one named last changes fastest.
Arguments:
- acts: bfloat16 [4, 4, 8, 6, 10240], P('section', 'batch', 'tm'), may hold values from -6 to 6
- cot: bfloat16 [4, 8, 6, 10240], P('batch', 'tm'), may hold values from -6 to 6
- spatial_weight: bfloat16 [4, 9, 64, 64], P('section'), may hold values from -0.25 to 0.25
- temporal_weight: bfloat16 [4, 3, 64, 64], P('section'), may hold values from -0.4375 to 0.4375
Outputs:
- grad_in: bfloat16 [4, 4, 8, 6, 10240], P('section', 'batch', 'tm')
- grad_spatial: float32 [4, 9, 64, 64], P('section')
- grad_temporal: float32 [4, 3, 64, 64], P('section')
All inputs are finite; a program needn't handle non-finite values.
Results may differ from a plain program's by a relative error of at most 0.012.
Values may be sent and summed in bfloat16 or wider, within the bound.
A program may use at most 128 MiB of HBM per device.

v0:
```python
import jax
import jax.numpy as jnp
from jax import lax
from jax.sharding import PartitionSpec as P

TIME_DILATION = 2


def from_behind(value, axis, steps):
    count = lax.axis_size(axis)
    first, last = (max(0, -steps), min(count, count - steps))
    return lax.ppermute(value, axis, [(source, source + steps) for source in range(first, last)])


def split_pixels(a, chans):
    return a.reshape(a.shape[:-1] + (a.shape[-1] // chans, chans))


def paired_kernel(kernel):
    return jnp.kron(jnp.eye(2, dtype=kernel.dtype), kernel)


def spatial_fwd(x, ws):
    rows, width = (x.shape[1], x.shape[2])
    chans = ws.shape[-1]
    padded = jnp.pad(x, ((0, 0), (1, 1), (chans, chans)))
    total = jnp.zeros(x.shape, jnp.float32)
    for i in range(3):
        for j in range(3):
            piece = split_pixels(padded[:, i : i + rows, j * chans : j * chans + width], 2 * chans)
            total = total + jnp.einsum(
                "nrpa,ab->nrpb",
                piece,
                paired_kernel(ws[3 * i + j]),
                preferred_element_type=jnp.float32,
            ).reshape(x.shape)
    return total


def spatial_back(gz, x, ws):
    rows, width = (x.shape[1], x.shape[2])
    chans = ws.shape[-1]
    xpad = jnp.pad(x, ((0, 0), (1, 1), (chans, chans)))
    gradient_padded = jnp.pad(gz, ((0, 0), (1, 1), (chans, chans)))
    gz_pairs = split_pixels(gz, 2 * chans)
    total = jnp.zeros(x.shape, jnp.float32)
    grads = []
    for i in range(3):
        for j in range(3):
            gpiece = split_pixels(
                gradient_padded[:, 2 - i : 2 - i + rows, (2 - j) * chans : (2 - j) * chans + width],
                2 * chans,
            )
            total = total + jnp.einsum(
                "nrpb,ab->nrpa",
                gpiece,
                paired_kernel(ws[3 * i + j]),
                preferred_element_type=jnp.float32,
            ).reshape(x.shape)
            xpiece = split_pixels(xpad[:, i : i + rows, j * chans : j * chans + width], 2 * chans)
            square = jnp.einsum(
                "nrpa,nrpb->ab", xpiece, gz_pairs, preferred_element_type=jnp.float32
            )
            grads.append(square[:chans, :chans] + square[chans:, chans:])
    return (total, jnp.stack(grads))


def temporal_back(h, gradient_piece, gradient_padded, dilation_step, wt):
    count = gradient_piece.shape[0]
    chans = wt.shape[-1]
    kernel_taps = [
        gradient_padded[2 * dilation_step : 2 * dilation_step + count],
        gradient_piece,
        gradient_padded[0:count],
    ]
    h_pix = split_pixels(h, chans)
    gh = jnp.zeros(gradient_piece.shape, jnp.float32)
    tgrads = []
    for k in range(3):
        tap = split_pixels(kernel_taps[k], chans)
        gh = gh + jnp.einsum(
            "trwd,cd->trwc", tap, wt[k], preferred_element_type=jnp.float32
        ).reshape(gradient_piece.shape)
        tgrads.append(jnp.einsum("trwc,trwd->cd", h_pix, tap, preferred_element_type=jnp.float32))
    return (gh.astype(jnp.bfloat16), jnp.stack(tgrads))


def section_backward(x, gradient_piece, ws, wt):
    dilation_step = TIME_DILATION
    z = spatial_fwd(x, ws)
    sig = jax.nn.sigmoid(z)
    h = (z * sig).astype(jnp.bfloat16)
    deriv = sig * (1.0 + z * (1.0 - sig))
    tile_gradient, h_tile = (
        lax.all_to_all(gradient_piece, "tm", split_axis=2, concat_axis=0, tiled=True),
        lax.all_to_all(h, "tm", split_axis=2, concat_axis=0, tiled=True),
    )
    gradient_padded = jnp.pad(tile_gradient, ((dilation_step, dilation_step), (0, 0), (0, 0)))
    gh_tile, tgrads = temporal_back(h_tile, tile_gradient, gradient_padded, dilation_step, wt)
    gh = lax.all_to_all(gh_tile, "tm", split_axis=0, concat_axis=2, tiled=True)
    gz = (gh.astype(jnp.float32) * deriv).astype(jnp.bfloat16)
    back, sgrads = spatial_back(gz, x, ws)
    result = (gradient_piece.astype(jnp.float32) + back).astype(jnp.bfloat16)
    return (result, sgrads, tgrads)


def body(acts, cot, spatial_weight, temporal_weight):
    section_idx = lax.axis_index("section")
    number_sections = lax.axis_size("section")
    micro = acts.shape[1]
    local_acts = acts[0]
    ws = spatial_weight[0]
    wt = temporal_weight[0]
    received = jnp.zeros(cot.shape[1:], jnp.bfloat16)
    grads_in = jnp.zeros(local_acts.shape, jnp.bfloat16)
    acc_spatial = jnp.zeros(ws.shape, jnp.float32)
    acc_temporal = jnp.zeros(wt.shape, jnp.float32)
    total_turns = micro + number_sections - 1
    for turn in range(total_turns):
        which = jnp.int32(turn) - (number_sections - 1 - section_idx)
        valid = jnp.logical_and(which >= 0, which < micro)
        clipped = jnp.clip(which, 0, micro - 1)
        x_now = lax.dynamic_index_in_dim(local_acts, clipped, 0, keepdims=False)
        top_grad = lax.dynamic_index_in_dim(cot, clipped, 0, keepdims=False)
        incoming = jnp.where(section_idx == number_sections - 1, top_grad, received)
        result, sgrads, tgrads = section_backward(x_now, incoming, ws, wt)
        weight = valid.astype(jnp.float32)
        acc_spatial = acc_spatial + weight * sgrads
        acc_temporal = acc_temporal + weight * tgrads
        select = (jnp.arange(micro, dtype=jnp.int32) == which)[:, None, None, None]
        grads_in = jnp.where(select, result[None], grads_in)
        if turn + 1 < total_turns:
            received = from_behind(result, "section", -1)
    sum_spatial, sum_temporal = lax.psum((acc_spatial, acc_temporal), ("tm", "batch"))
    return (grads_in[None], sum_spatial[None], sum_temporal[None])


def solution(mesh):
    in_specs = (
        P("section", "batch", "tm", None, None),
        P("batch", "tm", None, None),
        P("section", None, None, None),
        P("section", None, None, None),
    )
    out_specs = (
        P("section", "batch", "tm", None, None),
        P("section", None, None, None),
        P("section", None, None, None),
    )
    return jax.shard_map(body, mesh=mesh, in_specs=in_specs, out_specs=out_specs, check_vma=False)
```

profile of v0, /device:TPU:24, one launch (start us, length us, event | category | flops | bytes accessed | tf_op | source)
XLA Modules:
  0.0 929.5 jit_solution(14927379624928204376)
XLA Ops:
  8.3 8.2 copy.623
  16.6 10.0 %reshape.1685 = bf16[4,2,15360]{2,1,0:T(2,128)(2,1)} reshape(bf16[10240,2,6]{2,1,0:T(2,128)(2,1)} %bitcast.1159) | data formatting | bytes 491520
  26.5 4.2 all-to-all-start
  75.6 3.3 pad_slice_fusion.50
  90.9 3.1 pad_slice_fusion.18
  126.4 13.6 %reshape.1686 = bf16[10240,2,6]{2,1,0:T(2,128)(2,1)} reshape(bf16[4,2,15360]{2,1,0:T(2,128)(2,1)} %all-to-all-done) | data formatting | bytes 491520
  140.0 10.6 %copy.624 = bf16[2,6,4,2560]{3,0,2,1:T(2,128)(2,1)S(1)} copy(bf16[2,6,4,2560]{1,0,3,2:T(2,128)(2,1)} %bitcast.1160) | data formatting | bytes 491520 | tf_op jit(solution)/shard_map/all_to_all | solution.py:95
  153.7 4.3 all-to-all-start.1
  159.1 4.6 all-to-all-done.1
  205.2 10.3 %copy.809 = bf16[2,6,10240]{1,0,2:T(2,128)(2,1)} copy(bf16[2,6,10240]{2,0,1:T(2,128)(2,1)} %get-tuple-element.11) | data formatting | bytes 491520 | tf_op jit(solution)/shard_map/convert_element_type | solution.py:92
  215.5 9.9 %reshape.1695 = bf16[4,2,15360]{2,1,0:T(2,128)(2,1)} reshape(bf16[10240,2,6]{2,1,0:T(2,128)(2,1)} %bitcast.1161) | data formatting | bytes 491520
  225.4 3.4 all-to-all-start.10
  233.9 8.2 copy.651
  242.1 9.9 %reshape.1687 = bf16[4,2,15360]{2,1,0:T(2,128)(2,1)} reshape(bf16[10240,2,6]{2,1,0:T(2,128)(2,1)} %bitcast.1175) | data formatting | bytes 491520
  252.0 4.2 all-to-all-start.2
  257.1 12.6 %reshape.1696 = bf16[10240,2,6]{2,1,0:T(2,128)(2,1)} reshape(bf16[4,2,15360]{2,1,0:T(2,128)(2,1)S(1)} %all-to-all-done.10) | data formatting | bytes 491520
  269.7 12.2 %copy.902 = bf16[2,6,4,2560]{3,2,0,1:T(4,128)(2,1)S(1)} copy(bf16[2,6,4,2560]{1,0,3,2:T(2,128)(2,1)} %bitcast.1162) | data formatting | bytes 491520 | tf_op jit(solution)/shard_map/all_to_all | solution.py:96
  283.3 12.6 %reshape.1688 = bf16[10240,2,6]{2,1,0:T(2,128)(2,1)} reshape(bf16[4,2,15360]{2,1,0:T(2,128)(2,1)S(1)} %all-to-all-done.2) | data formatting | bytes 491520
  296.0 10.2 %copy.652 = bf16[2,6,4,2560]{3,0,2,1:T(2,128)(2,1)S(1)} copy(bf16[2,6,4,2560]{1,0,3,2:T(2,128)(2,1)} %bitcast.1163) | data formatting | bytes 491520 | tf_op jit(solution)/shard_map/all_to_all | solution.py:95
  314.8 4.4 all-to-all-start.3
  321.1 3.8 all-to-all-done.3
  366.4 10.3 %copy.812 = bf16[2,6,10240]{1,0,2:T(2,128)(2,1)} copy(bf16[2,6,10240]{2,0,1:T(2,128)(2,1)} %get-tuple-element.9) | data formatting | bytes 491520 | tf_op jit(solution)/shard_map/convert_element_type | solution.py:92
  376.7 9.9 %reshape.1697 = bf16[4,2,15360]{2,1,0:T(2,128)(2,1)} reshape(bf16[10240,2,6]{2,1,0:T(2,128)(2,1)} %bitcast.1164) | data formatting | bytes 491520
  386.6 3.8 all-to-all-start.11
  395.5 8.1 copy.679
  403.7 9.9 %reshape.1689 = bf16[4,2,15360]{2,1,0:T(2,128)(2,1)} reshape(bf16[10240,2,6]{2,1,0:T(2,128)(2,1)} %bitcast.1176) | data formatting | bytes 491520
  413.6 4.2 all-to-all-start.4
  418.4 12.6 %reshape.1698 = bf16[10240,2,6]{2,1,0:T(2,128)(2,1)} reshape(bf16[4,2,15360]{2,1,0:T(2,128)(2,1)S(1)} %all-to-all-done.11) | data formatting | bytes 491520
  431.1 12.2 %copy.903 = bf16[2,6,4,2560]{3,2,0,1:T(4,128)(2,1)S(1)} copy(bf16[2,6,4,2560]{1,0,3,2:T(2,128)(2,1)} %bitcast.1165) | data formatting | bytes 491520 | tf_op jit(solution)/shard_map/all_to_all | solution.py:96
  444.7 12.6 %reshape.1690 = bf16[10240,2,6]{2,1,0:T(2,128)(2,1)} reshape(bf16[4,2,15360]{2,1,0:T(2,128)(2,1)S(1)} %all-to-all-done.4) | data formatting | bytes 491520
  457.3 10.2 %copy.680 = bf16[2,6,4,2560]{3,0,2,1:T(2,128)(2,1)S(1)} copy(bf16[2,6,4,2560]{1,0,3,2:T(2,128)(2,1)} %bitcast.1166) | data formatting | bytes 491520 | tf_op jit(solution)/shard_map/all_to_all | solution.py:95
  476.2 4.4 all-to-all-start.5
  482.3 3.8 all-to-all-done.5
  525.7 10.2 %copy.815 = bf16[2,6,10240]{1,0,2:T(2,128)(2,1)} copy(bf16[2,6,10240]{2,0,1:T(2,128)(2,1)} %get-tuple-element.7) | data formatting | bytes 491520 | tf_op jit(solution)/shard_map/convert_element_type | solution.py:92
  536.0 9.9 %reshape.1699 = bf16[4,2,15360]{2,1,0:T(2,128)(2,1)} reshape(bf16[10240,2,6]{2,1,0:T(2,128)(2,1)} %bitcast.1167) | data formatting | bytes 491520
  545.9 3.6 all-to-all-start.12
  554.6 8.1 copy.707
  562.8 9.9 %reshape.1691 = bf16[4,2,15360]{2,1,0:T(2,128)(2,1)} reshape(bf16[10240,2,6]{2,1,0:T(2,128)(2,1)} %bitcast.1177) | data formatting | bytes 491520
  572.7 4.2 all-to-all-start.6
  577.8 12.6 %reshape.1700 = bf16[10240,2,6]{2,1,0:T(2,128)(2,1)} reshape(bf16[4,2,15360]{2,1,0:T(2,128)(2,1)S(1)} %all-to-all-done.12) | data formatting | bytes 491520
  590.4 12.2 %copy.904 = bf16[2,6,4,2560]{3,2,0,1:T(4,128)(2,1)S(1)} copy(bf16[2,6,4,2560]{1,0,3,2:T(2,128)(2,1)} %bitcast.1168) | data formatting | bytes 491520 | tf_op jit(solution)/shard_map/all_to_all | solution.py:96
  604.0 12.6 %reshape.1692 = bf16[10240,2,6]{2,1,0:T(2,128)(2,1)} reshape(bf16[4,2,15360]{2,1,0:T(2,128)(2,1)S(1)} %all-to-all-done.6) | data formatting | bytes 491520
  616.6 10.2 %copy.708 = bf16[2,6,4,2560]{3,0,2,1:T(2,128)(2,1)S(1)} copy(bf16[2,6,4,2560]{1,0,3,2:T(2,128)(2,1)} %bitcast.1169) | data formatting | bytes 491520 | tf_op jit(solution)/shard_map/all_to_all | solution.py:95
  635.5 4.6 all-to-all-start.7
  641.9 3.8 all-to-all-done.7
  687.6 10.2 %copy.818 = bf16[2,6,10240]{1,0,2:T(2,128)(2,1)} copy(bf16[2,6,10240]{2,0,1:T(2,128)(2,1)} %get-tuple-element.5) | data formatting | bytes 491520 | tf_op jit(solution)/shard_map/convert_element_type | solution.py:92
  697.8 9.9 %reshape.1701 = bf16[4,2,15360]{2,1,0:T(2,128)(2,1)} reshape(bf16[10240,2,6]{2,1,0:T(2,128)(2,1)} %bitcast.1170) | data formatting | bytes 491520
  707.7 3.6 all-to-all-start.13
  712.9 8.1 copy.735
  721.1 9.9 %reshape.1693 = bf16[4,2,15360]{2,1,0:T(2,128)(2,1)} reshape(bf16[10240,2,6]{2,1,0:T(2,128)(2,1)} %bitcast.1178) | data formatting | bytes 491520
  731.0 4.2 all-to-all-start.8
  735.9 12.6 %reshape.1702 = bf16[10240,2,6]{2,1,0:T(2,128)(2,1)} reshape(bf16[4,2,15360]{2,1,0:T(2,128)(2,1)S(1)} %all-to-all-done.13) | data formatting | bytes 491520
  748.5 12.2 %copy.905 = bf16[2,6,4,2560]{3,2,0,1:T(4,128)(2,1)S(1)} copy(bf16[2,6,4,2560]{1,0,3,2:T(2,128)(2,1)} %bitcast.1171) | data formatting | bytes 491520 | tf_op jit(solution)/shard_map/all_to_all | solution.py:96
  762.1 12.6 %reshape.1694 = bf16[10240,2,6]{2,1,0:T(2,128)(2,1)} reshape(bf16[4,2,15360]{2,1,0:T(2,128)(2,1)S(1)} %all-to-all-done.8) | data formatting | bytes 491520
  774.7 10.2 %copy.736 = bf16[2,6,4,2560]{3,0,2,1:T(2,128)(2,1)S(1)} copy(bf16[2,6,4,2560]{1,0,3,2:T(2,128)(2,1)} %bitcast.1172) | data formatting | bytes 491520 | tf_op jit(solution)/shard_map/all_to_all | solution.py:95
  788.7 4.3 all-to-all-start.9
  795.0 3.5 all-to-all-done.9
  841.1 10.3 %copy.821 = bf16[2,6,10240]{1,0,2:T(2,128)(2,1)} copy(bf16[2,6,10240]{2,0,1:T(2,128)(2,1)} %get-tuple-element.3) | data formatting | bytes 491520 | tf_op jit(solution)/shard_map/convert_element_type | solution.py:92
  851.4 9.9 %reshape.1703 = bf16[4,2,15360]{2,1,0:T(2,128)(2,1)} reshape(bf16[10240,2,6]{2,1,0:T(2,128)(2,1)} %bitcast.1173) | data formatting | bytes 491520
  861.3 3.6 all-to-all-start.14
  866.9 3.6 all-to-all-done.14
  870.4 12.6 %reshape.1704 = bf16[10240,2,6]{2,1,0:T(2,128)(2,1)} reshape(bf16[4,2,15360]{2,1,0:T(2,128)(2,1)S(1)} %all-to-all-done.14) | data formatting | bytes 491520
  883.2 12.3 %copy.906 = bf16[2,6,4,2560]{3,2,0,1:T(4,128)(2,1)S(1)} copy(bf16[2,6,4,2560]{1,0,3,2:T(2,128)(2,1)} %bitcast.1174) | data formatting | bytes 491520 | tf_op jit(solution)/shard_map/all_to_all | solution.py:96
  897.0 23.7 %psum.15 = f32[1,3,64,64]{3,2,1,0:T(8,128)} all-reduce(f32[1,3,64,64]{3,2,1,0:T(8,128)S(1)} %fusion.170), channel_id=1, replica_groups=mesh['section'=4,'tm'=4,'batch'=2] {'tm','batch'}, use_global_device_ids=true, to_apply=%region_1.2 | all-reduce | flops 12288 | bytes 98304 | tf_op jit(solution)/shard_map/psum | solution.py:134
  (796 shorter events, 366.7 us)
Async XLA Ops:
  8.3 24.1 %copy-start.132 = (bf16[1,9,64,64]{3,2,1,0:T(8,128)(2,1)S(1)}, bf16[1,9,64,64]{3,2,1,0:T(8,128)(2,1)}, u32[]{:S(2)}) copy-start(bf16[1,9,64,64]{3,2,1,0:T(8,128)(2,1)} %param.6) | copy-start | bytes 221188
  26.5 99.9 %all-to-all-start = ((bf16[4,2,15360]{2,1,0:T(2,128)(2,1)}), bf16[4,2,15360]{2,1,0:T(2,128)(2,1)}, u32[]{:S(2)}, u32[]{:S(2)}) async-start(bf16[4,2,15360]{2,1,0:T(2,128)(2,1)} %reshape.1685), calls=%async_computation | async-start | bytes 491520 | tf_op jit(solution)/shard_map/all_to_all | solution.py:95
  33.8 160.6 %copy-start.16 = (bf16[128,128,1,1]{1,0,2,3:T(8,128)(2,1)}, bf16[128,128,1,1]{1,0,2,3:T(8,128)(2,1)S(1)}, u32[]{:S(2)}) copy-start(bf16[128,128,1,1]{1,0,2,3:T(8,128)(2,1)S(1)} %reshape.1603) | copy-start | bytes 98308
  33.9 160.8 %copy-start.11 = (bf16[128,128,1,1]{1,0,2,3:T(8,128)(2,1)}, bf16[128,128,1,1]{1,0,2,3:T(8,128)(2,1)S(1)}, u32[]{:S(2)}) copy-start(bf16[128,128,1,1]{1,0,2,3:T(8,128)(2,1)S(1)} %reshape.1604) | copy-start | bytes 98308
  34.1 160.9 %copy-start.6 = (bf16[128,128,1,1]{1,0,2,3:T(8,128)(2,1)}, bf16[128,128,1,1]{1,0,2,3:T(8,128)(2,1)S(1)}, u32[]{:S(2)}) copy-start(bf16[128,128,1,1]{1,0,2,3:T(8,128)(2,1)S(1)} %reshape.1605) | copy-start | bytes 98308
  34.2 162.0 %copy-start.1 = (bf16[128,128,1,1]{1,0,2,3:T(8,128)(2,1)}, bf16[128,128,1,1]{1,0,2,3:T(8,128)(2,1)S(1)}, u32[]{:S(2)}) copy-start(bf16[128,128,1,1]{1,0,2,3:T(8,128)(2,1)S(1)} %reshape.1606) | copy-start | bytes 98308
  34.6 159.6 %copy-start.21 = (bf16[128,128,1,1]{1,0,2,3:T(8,128)(2,1)}, bf16[128,128,1,1]{1,0,2,3:T(8,128)(2,1)S(1)}, u32[]{:S(2)}) copy-start(bf16[128,128,1,1]{1,0,2,3:T(8,128)(2,1)S(1)} %reshape.1602) | copy-start | bytes 98308
  35.7 90.1 %copy-start.43 = (bf16[2,6,80,128]{3,2,0,1:T(8,128)(2,1)}, bf16[2,6,80,128]{3,2,0,1:T(8,128)(2,1)S(1)}, u32[]{:S(2)}) copy-start(bf16[2,6,80,128]{3,2,0,1:T(8,128)(2,1)S(1)} %reshape.1505) | copy-start | bytes 737284
  153.7 9.9 %all-to-all-start.1 = ((bf16[8,6,2560]{2,1,0:T(8,128)(2,1)}), bf16[8,6,2560]{2,1,0:T(8,128)(2,1)S(1)}, u32[]{:S(2)}, u32[]{:S(2)}) async-start(bf16[8,6,2560]{2,1,0:T(8,128)(2,1)} %reshape.1671), calls=%async_computation.1 | async-start | bytes 655360 | tf_op jit(solution)/shard_map/all_to_all | solution.py:100
  202.7 31.0 %collective-permute-start = (bf16[2,6,10240]{2,0,1:T(2,128)(2,1)S(1)}, bf16[2,6,10240]{2,0,1:T(2,128)(2,1)S(1)}, u32[]{:S(2)}, u32[]{:S(2)}) collective-permute-start(bf16[2,6,10240]{2,0,1:T(2,128)(2,1)S(1)} %add_convert_fusion.5), channel_id=1, source_target_pairs={{8,0},{16,8},{24,16},{9,1},{17,9},{25,17},{10,2},{18,10},{26,18},{... | collective-permute-start | bytes 737288 | tf_op jit(solution)/shard_map/ppermute | solution.py:12
  205.1 23.7 %copy-start.170 = (f32[128,128]{1,0:T(8,128)S(1)}, f32[128,128]{1,0:T(8,128)}, u32[]{:S(2)}) copy-start(f32[128,128]{1,0:T(8,128)} %convolution_bitcast_fusion.43) | copy-start | bytes 196612
  205.1 24.4 %copy-start.166 = (f32[128,128]{1,0:T(8,128)S(1)}, f32[128,128]{1,0:T(8,128)}, u32[]{:S(2)}) copy-start(f32[128,128]{1,0:T(8,128)} %convolution_bitcast_fusion.42) | copy-start | bytes 196612
  205.1 25.1 %copy-start.162 = (f32[128,128]{1,0:T(8,128)S(1)}, f32[128,128]{1,0:T(8,128)}, u32[]{:S(2)}) copy-start(f32[128,128]{1,0:T(8,128)} %convolution_bitcast_fusion.41) | copy-start | bytes 196612
  205.1 25.7 %copy-start.158 = (f32[128,128]{1,0:T(8,128)S(1)}, f32[128,128]{1,0:T(8,128)}, u32[]{:S(2)}) copy-start(f32[128,128]{1,0:T(8,128)} %convolution_bitcast_fusion.40) | copy-start | bytes 196612
  205.1 26.4 %copy-start.154 = (f32[128,128]{1,0:T(8,128)S(1)}, f32[128,128]{1,0:T(8,128)}, u32[]{:S(2)}) copy-start(f32[128,128]{1,0:T(8,128)} %convolution_bitcast_fusion.39) | copy-start | bytes 196612
  205.1 27.1 %copy-start.150 = (f32[128,128]{1,0:T(8,128)S(1)}, f32[128,128]{1,0:T(8,128)}, u32[]{:S(2)}) copy-start(f32[128,128]{1,0:T(8,128)} %convolution_bitcast_fusion.38) | copy-start | bytes 196612
  205.1 27.8 %copy-start.149 = (f32[128,128]{1,0:T(8,128)S(1)}, f32[128,128]{1,0:T(8,128)}, u32[]{:S(2)}) copy-start(f32[128,128]{1,0:T(8,128)} %convolution_bitcast_fusion.37) | copy-start | bytes 196612
  225.4 26.6 %all-to-all-start.10 = ((bf16[4,2,15360]{2,1,0:T(2,128)(2,1)}), bf16[4,2,15360]{2,1,0:T(2,128)(2,1)S(1)}, u32[]{:S(2)}, u32[]{:S(2)}) async-start(bf16[4,2,15360]{2,1,0:T(2,128)(2,1)} %reshape.1695), calls=%async_computation.10 | async-start | bytes 491520 | tf_op jit(solution)/shard_map/all_to_all | solution.py:96
  252.0 31.3 %all-to-all-start.2 = ((bf16[4,2,15360]{2,1,0:T(2,128)(2,1)}), bf16[4,2,15360]{2,1,0:T(2,128)(2,1)S(1)}, u32[]{:S(2)}, u32[]{:S(2)}) async-start(bf16[4,2,15360]{2,1,0:T(2,128)(2,1)} %reshape.1687), calls=%async_computation.2 | async-start | bytes 491520 | tf_op jit(solution)/shard_map/all_to_all | solution.py:95
  314.8 10.0 %all-to-all-start.3 = ((bf16[8,6,2560]{2,1,0:T(8,128)(2,1)}), bf16[8,6,2560]{2,1,0:T(8,128)(2,1)}, u32[]{:S(2)}, u32[]{:S(2)}) async-start(bf16[8,6,2560]{2,1,0:T(8,128)(2,1)} %reshape.1681), calls=%async_computation.3 | async-start | bytes 655360 | tf_op jit(solution)/shard_map/all_to_all | solution.py:100
  364.0 22.6 %copy-start.105 = (bf16[2,6,10240]{2,0,1:T(2,128)(2,1)}, bf16[2,6,10240]{2,0,1:T(2,128)(2,1)S(1)}, u32[]{:S(2)}) copy-start(bf16[2,6,10240]{2,0,1:T(2,128)(2,1)S(1)} %add_convert_fusion.4) | copy-start | bytes 737284
  364.0 31.2 %collective-permute-start.1 = (bf16[2,6,10240]{2,0,1:T(2,128)(2,1)S(1)}, bf16[2,6,10240]{2,0,1:T(2,128)(2,1)S(1)}, u32[]{:S(2)}, u32[]{:S(2)}) collective-permute-start(bf16[2,6,10240]{2,0,1:T(2,128)(2,1)S(1)} %add_convert_fusion.4), channel_id=1, source_target_pairs={{8,0},{16,8},{24,16},{9,1},{17,9},{25,17},{10,2},{18,10},{26,18},{... | collective-permute-start | bytes 737288 | tf_op jit(solution)/shard_map/ppermute | solution.py:12
  366.4 24.0 %copy-start.172 = (f32[128,128]{1,0:T(8,128)S(1)}, f32[128,128]{1,0:T(8,128)}, u32[]{:S(2)}) copy-start(f32[128,128]{1,0:T(8,128)} %convolution_bitcast_fusion.34) | copy-start | bytes 196612
  366.4 25.4 %copy-start.167 = (f32[128,128]{1,0:T(8,128)S(1)}, f32[128,128]{1,0:T(8,128)}, u32[]{:S(2)}) copy-start(f32[128,128]{1,0:T(8,128)} %convolution_bitcast_fusion.32) | copy-start | bytes 196612
  366.4 26.1 %copy-start.163 = (f32[128,128]{1,0:T(8,128)S(1)}, f32[128,128]{1,0:T(8,128)}, u32[]{:S(2)}) copy-start(f32[128,128]{1,0:T(8,128)} %convolution_bitcast_fusion.31) | copy-start | bytes 196612
  366.4 26.8 %copy-start.159 = (f32[128,128]{1,0:T(8,128)S(1)}, f32[128,128]{1,0:T(8,128)}, u32[]{:S(2)}) copy-start(f32[128,128]{1,0:T(8,128)} %convolution_bitcast_fusion.30) | copy-start | bytes 196612
  366.4 27.4 %copy-start.155 = (f32[128,128]{1,0:T(8,128)S(1)}, f32[128,128]{1,0:T(8,128)}, u32[]{:S(2)}) copy-start(f32[128,128]{1,0:T(8,128)} %convolution_bitcast_fusion.29) | copy-start | bytes 196612
  366.4 28.1 %copy-start.151 = (f32[128,128]{1,0:T(8,128)S(1)}, f32[128,128]{1,0:T(8,128)}, u32[]{:S(2)}) copy-start(f32[128,128]{1,0:T(8,128)} %convolution_bitcast_fusion.28) | copy-start | bytes 196612
  386.6 26.9 %all-to-all-start.11 = ((bf16[4,2,15360]{2,1,0:T(2,128)(2,1)}), bf16[4,2,15360]{2,1,0:T(2,128)(2,1)S(1)}, u32[]{:S(2)}, u32[]{:S(2)}) async-start(bf16[4,2,15360]{2,1,0:T(2,128)(2,1)} %reshape.1697), calls=%async_computation.11 | async-start | bytes 491520 | tf_op jit(solution)/shard_map/all_to_all | solution.py:96
  413.6 31.1 %all-to-all-start.4 = ((bf16[4,2,15360]{2,1,0:T(2,128)(2,1)}), bf16[4,2,15360]{2,1,0:T(2,128)(2,1)S(1)}, u32[]{:S(2)}, u32[]{:S(2)}) async-start(bf16[4,2,15360]{2,1,0:T(2,128)(2,1)} %reshape.1689), calls=%async_computation.4 | async-start | bytes 491520 | tf_op jit(solution)/shard_map/all_to_all | solution.py:95
  476.2 10.0 %all-to-all-start.5 = ((bf16[8,6,2560]{2,1,0:T(8,128)(2,1)}), bf16[8,6,2560]{2,1,0:T(8,128)(2,1)}, u32[]{:S(2)}, u32[]{:S(2)}) async-start(bf16[8,6,2560]{2,1,0:T(8,128)(2,1)} %reshape.1682), calls=%async_computation.5 | async-start | bytes 655360 | tf_op jit(solution)/shard_map/all_to_all | solution.py:100
  523.5 30.9 %collective-permute-start.2 = (bf16[2,6,10240]{2,0,1:T(2,128)(2,1)S(1)}, bf16[2,6,10240]{2,0,1:T(2,128)(2,1)S(1)}, u32[]{:S(2)}, u32[]{:S(2)}) collective-permute-start(bf16[2,6,10240]{2,0,1:T(2,128)(2,1)S(1)} %add_convert_fusion.3), channel_id=1, source_target_pairs={{8,0},{16,8},{24,16},{9,1},{17,9},{25,17},{10,2},{18,10},{26,18},{... | collective-permute-start | bytes 737288 | tf_op jit(solution)/shard_map/ppermute | solution.py:12
  525.7 23.8 %copy-start.173 = (f32[128,128]{1,0:T(8,128)S(1)}, f32[128,128]{1,0:T(8,128)}, u32[]{:S(2)}) copy-start(f32[128,128]{1,0:T(8,128)} %convolution_bitcast_fusion.25) | copy-start | bytes 196612
  525.7 25.2 %copy-start.169 = (f32[128,128]{1,0:T(8,128)S(1)}, f32[128,128]{1,0:T(8,128)}, u32[]{:S(2)}) copy-start(f32[128,128]{1,0:T(8,128)} %convolution_bitcast_fusion.23) | copy-start | bytes 196612
  525.7 25.9 %copy-start.165 = (f32[128,128]{1,0:T(8,128)S(1)}, f32[128,128]{1,0:T(8,128)}, u32[]{:S(2)}) copy-start(f32[128,128]{1,0:T(8,128)} %convolution_bitcast_fusion.22) | copy-start | bytes 196612
  525.7 26.6 %copy-start.161 = (f32[128,128]{1,0:T(8,128)S(1)}, f32[128,128]{1,0:T(8,128)}, u32[]{:S(2)}) copy-start(f32[128,128]{1,0:T(8,128)} %convolution_bitcast_fusion.21) | copy-start | bytes 196612
  525.7 27.2 %copy-start.157 = (f32[128,128]{1,0:T(8,128)S(1)}, f32[128,128]{1,0:T(8,128)}, u32[]{:S(2)}) copy-start(f32[128,128]{1,0:T(8,128)} %convolution_bitcast_fusion.20) | copy-start | bytes 196612
  525.7 27.9 %copy-start.153 = (f32[128,128]{1,0:T(8,128)S(1)}, f32[128,128]{1,0:T(8,128)}, u32[]{:S(2)}) copy-start(f32[128,128]{1,0:T(8,128)} %convolution_bitcast_fusion.19) | copy-start | bytes 196612
  545.9 26.8 %all-to-all-start.12 = ((bf16[4,2,15360]{2,1,0:T(2,128)(2,1)}), bf16[4,2,15360]{2,1,0:T(2,128)(2,1)S(1)}, u32[]{:S(2)}, u32[]{:S(2)}) async-start(bf16[4,2,15360]{2,1,0:T(2,128)(2,1)} %reshape.1699), calls=%async_computation.12 | async-start | bytes 491520 | tf_op jit(solution)/shard_map/all_to_all | solution.py:96
  572.7 31.3 %all-to-all-start.6 = ((bf16[4,2,15360]{2,1,0:T(2,128)(2,1)}), bf16[4,2,15360]{2,1,0:T(2,128)(2,1)S(1)}, u32[]{:S(2)}, u32[]{:S(2)}) async-start(bf16[4,2,15360]{2,1,0:T(2,128)(2,1)} %reshape.1691), calls=%async_computation.6 | async-start | bytes 491520 | tf_op jit(solution)/shard_map/all_to_all | solution.py:95
  635.5 10.2 %all-to-all-start.7 = ((bf16[8,6,2560]{2,1,0:T(8,128)(2,1)}), bf16[8,6,2560]{2,1,0:T(8,128)(2,1)}, u32[]{:S(2)}, u32[]{:S(2)}) async-start(bf16[8,6,2560]{2,1,0:T(8,128)(2,1)} %reshape.1683), calls=%async_computation.7 | async-start | bytes 655360 | tf_op jit(solution)/shard_map/all_to_all | solution.py:100
  685.6 27.1 %collective-permute-start.3 = (bf16[2,6,10240]{2,0,1:T(2,128)(2,1)S(1)}, bf16[2,6,10240]{2,0,1:T(2,128)(2,1)S(1)}, u32[]{:S(2)}, u32[]{:S(2)}) collective-permute-start(bf16[2,6,10240]{2,0,1:T(2,128)(2,1)S(1)} %add_convert_fusion.2), channel_id=1, source_target_pairs={{8,0},{16,8},{24,16},{9,1},{17,9},{25,17},{10,2},{18,10},{26,18},{... | collective-permute-start | bytes 737288 | tf_op jit(solution)/shard_map/ppermute | solution.py:12
  687.5 23.8 %copy-start.121 = (f32[9,64,64]{2,1,0:T(8,128)S(1)}, f32[9,64,64]{2,1,0:T(8,128)}, u32[]{:S(2)}) copy-start(f32[9,64,64]{2,1,0:T(8,128)} %constant_dynamic-update-slice_fusion.35) | copy-start | bytes 442372
  687.5 24.6 %copy-start.171 = (f32[128,128]{1,0:T(8,128)S(1)}, f32[128,128]{1,0:T(8,128)}, u32[]{:S(2)}) copy-start(f32[128,128]{1,0:T(8,128)} %convolution_bitcast_fusion.15) | copy-start | bytes 196612
  687.5 24.7 %copy-start.168 = (f32[128,128]{1,0:T(8,128)S(1)}, f32[128,128]{1,0:T(8,128)}, u32[]{:S(2)}) copy-start(f32[128,128]{1,0:T(8,128)} %convolution_bitcast_fusion.14) | copy-start | bytes 196612
  687.5 24.7 %copy-start.164 = (f32[128,128]{1,0:T(8,128)S(1)}, f32[128,128]{1,0:T(8,128)}, u32[]{:S(2)}) copy-start(f32[128,128]{1,0:T(8,128)} %convolution_bitcast_fusion.13) | copy-start | bytes 196612
  687.6 24.8 %copy-start.160 = (f32[128,128]{1,0:T(8,128)S(1)}, f32[128,128]{1,0:T(8,128)}, u32[]{:S(2)}) copy-start(f32[128,128]{1,0:T(8,128)} %convolution_bitcast_fusion.12) | copy-start | bytes 196612
  687.6 24.9 %copy-start.156 = (f32[128,128]{1,0:T(8,128)S(1)}, f32[128,128]{1,0:T(8,128)}, u32[]{:S(2)}) copy-start(f32[128,128]{1,0:T(8,128)} %convolution_bitcast_fusion.11) | copy-start | bytes 196612
  687.6 25.0 %copy-start.152 = (f32[128,128]{1,0:T(8,128)S(1)}, f32[128,128]{1,0:T(8,128)}, u32[]{:S(2)}) copy-start(f32[128,128]{1,0:T(8,128)} %convolution_bitcast_fusion.10) | copy-start | bytes 196612
  707.7 23.3 %all-to-all-start.13 = ((bf16[4,2,15360]{2,1,0:T(2,128)(2,1)}), bf16[4,2,15360]{2,1,0:T(2,128)(2,1)S(1)}, u32[]{:S(2)}, u32[]{:S(2)}) async-start(bf16[4,2,15360]{2,1,0:T(2,128)(2,1)} %reshape.1701), calls=%async_computation.13 | async-start | bytes 491520 | tf_op jit(solution)/shard_map/all_to_all | solution.py:96
  731.0 31.1 %all-to-all-start.8 = ((bf16[4,2,15360]{2,1,0:T(2,128)(2,1)}), bf16[4,2,15360]{2,1,0:T(2,128)(2,1)S(1)}, u32[]{:S(2)}, u32[]{:S(2)}) async-start(bf16[4,2,15360]{2,1,0:T(2,128)(2,1)} %reshape.1693), calls=%async_computation.8 | async-start | bytes 491520 | tf_op jit(solution)/shard_map/all_to_all | solution.py:95
  735.9 24.8 %copy-start.122 = (f32[9,64,64]{2,1,0:T(8,128)}, f32[9,64,64]{2,1,0:T(8,128)S(1)}, u32[]{:S(2)}) copy-start(f32[9,64,64]{2,1,0:T(8,128)S(1)} %get-tuple-element.143) | copy-start | bytes 442372
  788.7 9.9 %all-to-all-start.9 = ((bf16[8,6,2560]{2,1,0:T(8,128)(2,1)}), bf16[8,6,2560]{2,1,0:T(8,128)(2,1)S(1)}, u32[]{:S(2)}, u32[]{:S(2)}) async-start(bf16[8,6,2560]{2,1,0:T(8,128)(2,1)} %reshape.1684), calls=%async_computation.9 | async-start | bytes 655360 | tf_op jit(solution)/shard_map/all_to_all | solution.py:100
  793.0 127.7 %all-reduce.17.cloned.1.call-start = ((), (), s32[]{:S(2)}) async-start(), calls=%async_computation.15 | async-start | bytes 589824 | tf_op jit(solution)/shard_map/psum | solution.py:134
  841.0 24.0 %copy-start.53 = (bf16[2,6,10240]{2,0,1:T(2,128)(2,1)S(1)}, bf16[2,6,10240]{2,0,1:T(2,128)(2,1)}, u32[]{:S(2)}) copy-start(bf16[2,6,10240]{2,0,1:T(2,128)(2,1)} %fusion.25) | copy-start | bytes 737284
  841.1 24.0 %copy-start.106 = (bf16[2,6,10240]{2,0,1:T(2,128)(2,1)S(1)}, bf16[2,6,10240]{2,0,1:T(2,128)(2,1)}, u32[]{:S(2)}) copy-start(bf16[2,6,10240]{2,0,1:T(2,128)(2,1)} %copy-done.105) | copy-start | bytes 737284
  841.1 24.0 %copy-start.108 = (bf16[2,6,10240]{2,0,1:T(2,128)(2,1)S(1)}, bf16[2,6,10240]{2,0,1:T(2,128)(2,1)}, u32[]{:S(2)}) copy-start(bf16[2,6,10240]{2,0,1:T(2,128)(2,1)} %copy-done.107) | copy-start | bytes 737284
  841.1 24.0 %copy-start.110 = (bf16[2,6,10240]{2,0,1:T(2,128)(2,1)S(1)}, bf16[2,6,10240]{2,0,1:T(2,128)(2,1)}, u32[]{:S(2)}) copy-start(bf16[2,6,10240]{2,0,1:T(2,128)(2,1)} %copy-done.109) | copy-start | bytes 737284
  841.1 24.0 %copy-start.174 = (pred[2]{0:T(512)(128)(4,1)S(1)}, pred[2]{0:T(512)(128)(4,1)}, u32[]{:S(2)}) copy-start(pred[2]{0:T(512)(128)(4,1)} %get-tuple-element.138) | copy-start | bytes 10
  841.1 24.0 %copy-start.175 = (pred[2]{0:T(512)(128)(4,1)S(1)}, pred[2]{0:T(512)(128)(4,1)}, u32[]{:S(2)}) copy-start(pred[2]{0:T(512)(128)(4,1)} %get-tuple-element.139) | copy-start | bytes 10
  841.1 24.0 %copy-start.176 = (pred[2]{0:T(512)(128)(4,1)S(1)}, pred[2]{0:T(512)(128)(4,1)}, u32[]{:S(2)}) copy-start(pred[2]{0:T(512)(128)(4,1)} %get-tuple-element.136) | copy-start | bytes 10
  841.1 24.0 %copy-start.177 = (pred[2]{0:T(512)(128)(4,1)S(1)}, pred[2]{0:T(512)(128)(4,1)}, u32[]{:S(2)}) copy-start(pred[2]{0:T(512)(128)(4,1)} %get-tuple-element.137) | copy-start | bytes 10
  841.1 24.0 %copy-start.178 = (pred[2]{0:T(512)(128)(4,1)S(1)}, pred[2]{0:T(512)(128)(4,1)}, u32[]{:S(2)}) copy-start(pred[2]{0:T(512)(128)(4,1)} %iota_compare_fusion.4) | copy-start | bytes 10
  861.3 9.1 all-to-all-start.14
  (135 other events, 1551.2 us)
Sparse Core Ops, SparseCore 0:
  820.6 53.1 all-reduce.16
where the time goes:
time: 944 us; the launch traced here: 930 us
  local copies, waits for them, and re-layouts  609 us (65%)
  matrix products  137 us (15%)
  starting transfers between devices  70 us (7%)
  other arithmetic  49 us (5%)
  blocking collectives  23.7 us (3%)
  waiting for transfers between devices  23.2 us (2%)
  between operations  17.9 us (2%)
    unnamed x379, local copies, waits for them, and re-layouts  229 us
    reshape x105, local copies, waits for them, and re-layouts, split_pixels(): return a.reshape(a.shape[:-1] + (a.shape[-1] // chans, chans))  112 us
    all_to_all x10, local copies, waits for them, and re-layouts, section_backward(): lax.all_to_all(h, 'tm', split_axis=2, concat_axis=0, tiled=True)  61.8 us
    dot_general x45, matrix products, spatial_back(): jnp.einsum('nrpa,nrpb->ab', xpiece, gz_pairs, preferred_element_type=jnp....  54.5 us
    all_to_all x10, local copies, waits for them, and re-layouts, section_backward(): lax.all_to_all(gradient_piece, 'tm', split_axis=2, concat_axis=0, tiled=T...  52.1 us
    convert_element_type x5, local copies, waits for them, and re-layouts, section_backward(): h = (z * sig).astype(jnp.bfloat16)  51.3 us
    select_n x5, local copies, waits for them, and re-layouts, body(): incoming = jnp.where(section_idx == number_sections - 1, top_grad, received)  40.8 us
    dot_general x45, matrix products, spatial_fwd(): jnp.einsum('nrpa,ab->nrpb', piece, paired_kernel(ws[3 * i + j]), preferre...  28.6 us
  transfers between devices with their start and end apart: 20, of which 6 were waited for; matrix products, arithmetic and copies ran while one was open for 48% of the time, Pallas kernels for 0%

commit v1 on v0

--- a/solution.py
+++ b/solution.py
@@ -2,8 +2,22 @@
 import jax.numpy as jnp
 from jax import lax
 from jax.sharding import PartitionSpec as P
+from jax.lax import axis_index, ppermute, psum
 
 TIME_DILATION = 2
+
+
+def _read_shelves(packet, along_dim, m):
+    taken_in, far_arr = (packet.shape[:along_dim], packet.shape[along_dim + 1 :])
+    return jnp.moveaxis(packet.reshape(*taken_in, m, -1, *far_arr), along_dim, 0)
+
+
+def draft_keys(load, dimension_no):
+    load = jnp.moveaxis(load, 0, dimension_no)
+    z2 = load.shape
+    return load.reshape(
+        *z2[:dimension_no], z2[dimension_no] * z2[dimension_no + 1], *z2[dimension_no + 2 :]
+    )
 
 
 def from_behind(value, axis, steps):
@@ -91,9 +105,23 @@
     sig = jax.nn.sigmoid(z)
     h = (z * sig).astype(jnp.bfloat16)
     deriv = sig * (1.0 + z * (1.0 - sig))
+
+    def treat_lane(local, net_axis, arr, inputs):
+        formed, b_now = (psum(1, net_axis), axis_index(net_axis))
+        block_next = _read_shelves(local, arr, formed)
+        left_arr = block_next
+        for rr in range(1, formed):
+            carry_out, block_last = ((b_now + rr) % formed, (b_now - rr) % formed)
+            f_now = lax.dynamic_index_in_dim(block_next, carry_out, 0)
+            current_block = ppermute(
+                f_now, net_axis, perm=[(src_i, (src_i + rr) % formed) for src_i in range(formed)]
+            )
+            left_arr = lax.dynamic_update_slice_in_dim(left_arr, current_block, block_last, axis=0)
+        return draft_keys(left_arr, inputs)
+
     tile_gradient, h_tile = (
         lax.all_to_all(gradient_piece, "tm", split_axis=2, concat_axis=0, tiled=True),
-        lax.all_to_all(h, "tm", split_axis=2, concat_axis=0, tiled=True),
+        treat_lane(h, "tm", 2, 0),
     )
     gradient_padded = jnp.pad(tile_gradient, ((dilation_step, dilation_step), (0, 0), (0, 0)))
     gh_tile, tgrads = temporal_back(h_tile, tile_gradient, gradient_padded, dilation_step, wt)

time: 944 us -> 828 us (0.88)
  local copies, waits for them, and re-layouts: 609 us -> 446 us
  matrix products: 137 us -> 164 us
  other arithmetic: 49 us -> 73.6 us
    unnamed x379 -> x271, local copies, waits for them, and re-layouts: 229 us -> 117 us
    all_to_all x10 -> x0, local copies, waits for them, and re-layouts: 61.8 us -> none  [section_backward(): lax.all_to_all(h, 'tm', split_axis=2, concat_axis=0, tiled=True)]
    convert_element_type x5 -> x0, local copies, waits for them, and re-layouts: 51.3 us -> none  [section_backward(): h = (z * sig).astype(jnp.bfloat16)]
    dynamic_update_slice x0 -> x20, local copies, waits for them, and re-layouts: none -> 41.7 us  [treat_lane(): lax.dynamic_update_slice_in_dim(left_arr, current_block, block_last, axis=0)]
    dot_general x45, matrix products: 54.5 us -> 78.8 us  [spatial_back(): jnp.einsum('nrpa,nrpb->ab', xpiece, gz_pairs, preferred_element_type=jnp....]
    all_to_all x5 -> x0, starting transfers between devices: 18 us -> none  [section_backward(): lax.all_to_all(h, 'tm', split_axis=2, concat_axis=0, tiled=True)]
    unnamed x40, other arithmetic: 24.6 us -> 42.6 us
    ppermute x0 -> x15, starting transfers between devices: none -> 17.9 us  [treat_lane(): ppermute(f_now, net_axis, perm=[(src_i, (src_i + rr) % formed) for src_i...]
  transfers between devices with their start and end apart: 20 -> 30, of which waited for: 6 -> 5; matrix products, arithmetic and copies ran while one was open for 48% -> 44% of each run, Pallas kernels for 0% -> 0%
where the time goes in v1:
time: 828 us; the launch traced here: 814 us
  local copies, waits for them, and re-layouts  446 us (54%)
  matrix products  164 us (20%)
  other arithmetic  73.6 us (9%)
  starting transfers between devices  68.6 us (8%)
  blocking collectives  23.8 us (3%)
  waiting for transfers between devices  19.8 us (2%)
  between operations  17.6 us (2%)
    unnamed x271, local copies, waits for them, and re-layouts  117 us
    reshape x100, local copies, waits for them, and re-layouts, split_pixels(): return a.reshape(a.shape[:-1] + (a.shape[-1] // chans, chans))  116 us
    dot_general x45, matrix products, spatial_back(): jnp.einsum('nrpa,nrpb->ab', xpiece, gz_pairs, preferred_element_type=jnp....  78.8 us
    all_to_all x10, local copies, waits for them, and re-layouts, section_backward(): lax.all_to_all(gradient_piece, 'tm', split_axis=2, concat_axis=0, tiled=T...  51.9 us
    unnamed x40, other arithmetic  42.6 us
    dynamic_update_slice x20, local copies, waits for them, and re-layouts, treat_lane(): lax.dynamic_update_slice_in_dim(left_arr, current_block, block_last, axis=0)  41.7 us
    select_n x5, local copies, waits for them, and re-layouts, body(): incoming = jnp.where(section_idx == number_sections - 1, top_grad, received)  40.9 us
    dot_general x45, matrix products, spatial_fwd(): jnp.einsum('nrpa,ab->nrpb', piece, paired_kernel(ws[3 * i + j]), preferre...  31 us
  transfers between devices with their start and end apart: 30, of which 5 were waited for; matrix products, arithmetic and copies ran while one was open for 44% of the time, Pallas kernels for 0%

profile of v1, /device:TPU:24, one launch (start us, length us, event | category | flops | bytes accessed | tf_op | source)
XLA Modules:
  0.0 813.7 jit_solution(13957715892240514445)
XLA Ops:
  8.3 8.2 %copy.603 = bf16[2,6,10240]{1,0,2:T(2,128)(2,1)} copy(bf16[2,6,10240]{2,0,1:T(2,128)(2,1)S(1)} %fusion.326) | data formatting | bytes 491520 | tf_op jit(solution)/shard_map/jit(_where)/select_n | solution.py:153
  16.5 10.0 %reshape.1825 = bf16[4,2,15360]{2,1,0:T(2,128)(2,1)} reshape(bf16[10240,2,6]{2,1,0:T(2,128)(2,1)} %bitcast.1189) | data formatting | bytes 491520
  26.5 4.6 all-to-all-start
  37.8 2.9 pad_slice_fusion.34
  48.8 3.0 pad_slice_fusion.82
  60.2 3.0 pad_slice_fusion.66
  74.4 3.2 pad_slice_fusion.50
  89.6 3.1 pad_slice_fusion.18
  126.4 13.6 %reshape.1826 = bf16[10240,2,6]{2,1,0:T(2,128)(2,1)} reshape(bf16[4,2,15360]{2,1,0:T(2,128)(2,1)} %all-to-all-done) | data formatting | bytes 491520
  140.1 10.5 %copy.604 = bf16[2,6,4,2560]{3,0,2,1:T(2,128)(2,1)S(1)} copy(bf16[2,6,4,2560]{1,0,3,2:T(2,128)(2,1)} %bitcast.1190) | data formatting | bytes 491520 | tf_op jit(solution)/shard_map/all_to_all | solution.py:123
  153.5 4.2 all-to-all-start.1
  158.7 4.6 all-to-all-done.1
  186.5 2.9 pad_slice_fusion.74
  211.1 2.4 collective-permute-start
  221.1 8.2 %copy.631 = bf16[2,6,10240]{1,0,2:T(2,128)(2,1)} copy(bf16[2,6,10240]{2,0,1:T(2,128)(2,1)S(1)} %broadcast_select_fusion.9) | data formatting | bytes 491520 | tf_op jit(solution)/shard_map/jit(_where)/select_n | solution.py:153
  229.2 9.9 %reshape.1827 = bf16[4,2,15360]{2,1,0:T(2,128)(2,1)} reshape(bf16[10240,2,6]{2,1,0:T(2,128)(2,1)} %bitcast.1195) | data formatting | bytes 491520
  239.1 3.6 all-to-all-start.2
  243.7 2.7 dynamic_update_slice.45
  246.4 2.7 dynamic_update_slice.46
  249.1 2.7 dynamic_update_slice.47
  253.3 12.6 %reshape.1828 = bf16[10240,2,6]{2,1,0:T(2,128)(2,1)} reshape(bf16[4,2,15360]{2,1,0:T(2,128)(2,1)S(1)} %all-to-all-done.2) | data formatting | bytes 491520
  265.9 10.2 %copy.632 = bf16[2,6,4,2560]{3,0,2,1:T(2,128)(2,1)S(1)} copy(bf16[2,6,4,2560]{1,0,3,2:T(2,128)(2,1)} %bitcast.1191) | data formatting | bytes 491520 | tf_op jit(solution)/shard_map/all_to_all | solution.py:123
  284.8 4.4 all-to-all-start.3
  291.0 3.8 all-to-all-done.3
  327.7 3.1 pad_slice_fusion.58
  351.4 2.6 collective-permute-start.1
  362.2 8.2 %copy.659 = bf16[2,6,10240]{1,0,2:T(2,128)(2,1)} copy(bf16[2,6,10240]{2,0,1:T(2,128)(2,1)S(1)} %broadcast_select_fusion.8) | data formatting | bytes 491520 | tf_op jit(solution)/shard_map/jit(_where)/select_n | solution.py:153
  370.4 9.9 %reshape.1829 = bf16[4,2,15360]{2,1,0:T(2,128)(2,1)} reshape(bf16[10240,2,6]{2,1,0:T(2,128)(2,1)} %bitcast.1196) | data formatting | bytes 491520
  380.3 3.7 all-to-all-start.4
  384.7 2.7 dynamic_update_slice.48
  387.4 2.7 dynamic_update_slice.49
  390.1 2.7 dynamic_update_slice.50
  394.3 12.6 %reshape.1830 = bf16[10240,2,6]{2,1,0:T(2,128)(2,1)} reshape(bf16[4,2,15360]{2,1,0:T(2,128)(2,1)S(1)} %all-to-all-done.4) | data formatting | bytes 491520
  406.9 10.2 %copy.660 = bf16[2,6,4,2560]{3,0,2,1:T(2,128)(2,1)S(1)} copy(bf16[2,6,4,2560]{1,0,3,2:T(2,128)(2,1)} %bitcast.1192) | data formatting | bytes 491520 | tf_op jit(solution)/shard_map/all_to_all | solution.py:123
  425.8 4.6 all-to-all-start.5
  432.2 3.8 all-to-all-done.5
  467.1 3.1 pad_slice_fusion.42
  499.6 8.2 %copy.687 = bf16[2,6,10240]{1,0,2:T(2,128)(2,1)} copy(bf16[2,6,10240]{2,0,1:T(2,128)(2,1)S(1)} %broadcast_select_fusion.7) | data formatting | bytes 491520 | tf_op jit(solution)/shard_map/jit(_where)/select_n | solution.py:153
  507.7 9.9 %reshape.1831 = bf16[4,2,15360]{2,1,0:T(2,128)(2,1)} reshape(bf16[10240,2,6]{2,1,0:T(2,128)(2,1)} %bitcast.1197) | data formatting | bytes 491520
  517.6 3.7 all-to-all-start.6
  522.2 2.7 dynamic_update_slice.51
  524.9 2.7 dynamic_update_slice.52
  527.7 2.7 dynamic_update_slice.53
  531.8 12.6 %reshape.1832 = bf16[10240,2,6]{2,1,0:T(2,128)(2,1)} reshape(bf16[4,2,15360]{2,1,0:T(2,128)(2,1)S(1)} %all-to-all-done.6) | data formatting | bytes 491520
  544.4 10.2 %copy.688 = bf16[2,6,4,2560]{3,0,2,1:T(2,128)(2,1)S(1)} copy(bf16[2,6,4,2560]{1,0,3,2:T(2,128)(2,1)} %bitcast.1193) | data formatting | bytes 491520 | tf_op jit(solution)/shard_map/all_to_all | solution.py:123
  563.3 4.4 all-to-all-start.7
  569.5 3.8 all-to-all-done.7
  606.2 3.0 pad_slice_fusion.26
  641.9 8.2 %copy.715 = bf16[2,6,10240]{1,0,2:T(2,128)(2,1)} copy(bf16[2,6,10240]{2,0,1:T(2,128)(2,1)S(1)} %broadcast_select_fusion.6) | data formatting | bytes 491520 | tf_op jit(solution)/shard_map/jit(_where)/select_n | solution.py:153
  650.1 9.9 %reshape.1833 = bf16[4,2,15360]{2,1,0:T(2,128)(2,1)} reshape(bf16[10240,2,6]{2,1,0:T(2,128)(2,1)} %bitcast.1198) | data formatting | bytes 491520
  660.0 3.7 all-to-all-start.8
  664.4 2.7 dynamic_update_slice.54
  667.1 2.7 dynamic_update_slice.55
  669.9 2.7 dynamic_update_slice.56
  674.0 12.6 %reshape.1834 = bf16[10240,2,6]{2,1,0:T(2,128)(2,1)} reshape(bf16[4,2,15360]{2,1,0:T(2,128)(2,1)S(1)} %all-to-all-done.8) | data formatting | bytes 491520
  686.7 10.2 %copy.716 = bf16[2,6,4,2560]{3,0,2,1:T(2,128)(2,1)S(1)} copy(bf16[2,6,4,2560]{1,0,3,2:T(2,128)(2,1)} %bitcast.1194) | data formatting | bytes 491520 | tf_op jit(solution)/shard_map/all_to_all | solution.py:123
  700.6 4.3 all-to-all-start.9
  706.8 3.7 all-to-all-done.9
  747.3 3.0 pad_slice_fusion.10
  767.3 3.1 broadcast_select_fusion.3
  770.6 2.7 dynamic_update_slice.57
  773.4 2.7 dynamic_update_slice.58
  776.1 2.7 dynamic_update_slice.59
  781.2 23.8 %psum.15 = f32[1,3,64,64]{3,2,1,0:T(8,128)} all-reduce(f32[1,3,64,64]{3,2,1,0:T(8,128)S(1)} %fusion.175), channel_id=1, replica_groups=mesh['section'=4,'tm'=4,'batch'=2] {'tm','batch'}, use_global_device_ids=true, to_apply=%region_1.2 | all-reduce | flops 12288 | bytes 98304 | tf_op jit(solution)/shard_map/psum | solution.py:162
  (733 shorter events, 426.4 us)
Async XLA Ops:
  8.3 23.5 %copy-start.107 = (bf16[1,9,64,64]{3,2,1,0:T(8,128)(2,1)S(1)}, bf16[1,9,64,64]{3,2,1,0:T(8,128)(2,1)}, u32[]{:S(2)}) copy-start(bf16[1,9,64,64]{3,2,1,0:T(8,128)(2,1)} %param.6) | copy-start | bytes 221188
  26.5 100.0 %all-to-all-start = ((bf16[4,2,15360]{2,1,0:T(2,128)(2,1)}), bf16[4,2,15360]{2,1,0:T(2,128)(2,1)}, u32[]{:S(2)}, u32[]{:S(2)}) async-start(bf16[4,2,15360]{2,1,0:T(2,128)(2,1)} %reshape.1825), calls=%async_computation | async-start | bytes 491520 | tf_op jit(solution)/shard_map/all_to_all | solution.py:123
  32.5 132.2 %copy-start.37 = (bf16[128,128,1,1]{1,0,2,3:T(8,128)(2,1)}, bf16[128,128,1,1]{1,0,2,3:T(8,128)(2,1)S(1)}, u32[]{:S(2)}) copy-start(bf16[128,128,1,1]{1,0,2,3:T(8,128)(2,1)S(1)} %reshape.1750) | copy-start | bytes 98308
  32.6 164.7 %copy-start.16 = (bf16[128,128,1,1]{1,0,2,3:T(8,128)(2,1)}, bf16[128,128,1,1]{1,0,2,3:T(8,128)(2,1)S(1)}, u32[]{:S(2)}) copy-start(bf16[128,128,1,1]{1,0,2,3:T(8,128)(2,1)S(1)} %reshape.1743) | copy-start | bytes 98308
  32.7 165.9 %copy-start.11 = (bf16[128,128,1,1]{1,0,2,3:T(8,128)(2,1)}, bf16[128,128,1,1]{1,0,2,3:T(8,128)(2,1)S(1)}, u32[]{:S(2)}) copy-start(bf16[128,128,1,1]{1,0,2,3:T(8,128)(2,1)S(1)} %reshape.1744) | copy-start | bytes 98308
  32.8 166.0 %copy-start.6 = (bf16[128,128,1,1]{1,0,2,3:T(8,128)(2,1)}, bf16[128,128,1,1]{1,0,2,3:T(8,128)(2,1)S(1)}, u32[]{:S(2)}) copy-start(bf16[128,128,1,1]{1,0,2,3:T(8,128)(2,1)S(1)} %reshape.1745) | copy-start | bytes 98308
  32.9 166.1 %copy-start.1 = (bf16[128,128,1,1]{1,0,2,3:T(8,128)(2,1)}, bf16[128,128,1,1]{1,0,2,3:T(8,128)(2,1)S(1)}, u32[]{:S(2)}) copy-start(bf16[128,128,1,1]{1,0,2,3:T(8,128)(2,1)S(1)} %reshape.1746) | copy-start | bytes 98308
  33.3 163.7 %copy-start.21 = (bf16[128,128,1,1]{1,0,2,3:T(8,128)(2,1)}, bf16[128,128,1,1]{1,0,2,3:T(8,128)(2,1)S(1)}, u32[]{:S(2)}) copy-start(bf16[128,128,1,1]{1,0,2,3:T(8,128)(2,1)S(1)} %reshape.1742) | copy-start | bytes 98308
  34.4 91.3 %copy-start.43 = (bf16[2,6,80,128]{3,2,0,1:T(8,128)(2,1)}, bf16[2,6,80,128]{3,2,0,1:T(8,128)(2,1)S(1)}, u32[]{:S(2)}) copy-start(bf16[2,6,80,128]{3,2,0,1:T(8,128)(2,1)S(1)} %reshape.1610) | copy-start | bytes 737284
  95.6 29.5 %copy-start.44 = (bf16[2,6,80,128]{3,2,0,1:T(8,128)(2,1)}, bf16[2,6,80,128]{3,2,0,1:T(8,128)(2,1)S(1)}, u32[]{:S(2)}) copy-start(bf16[2,6,80,128]{3,2,0,1:T(8,128)(2,1)S(1)} %reshape.1607) | copy-start | bytes 737284
  153.5 9.8 %all-to-all-start.1 = ((bf16[8,6,2560]{2,1,0:T(8,128)(2,1)}), bf16[8,6,2560]{2,1,0:T(8,128)(2,1)S(1)}, u32[]{:S(2)}, u32[]{:S(2)}) async-start(bf16[8,6,2560]{2,1,0:T(8,128)(2,1)} %reshape.1811), calls=%async_computation.1 | async-start | bytes 655360 | tf_op jit(solution)/shard_map/all_to_all | solution.py:128
  205.9 43.2 %collective-permute-start.6 = (bf16[1,2,6,2560]{3,0,2,1:T(2,128)(2,1)}, bf16[1,2,6,2560]{3,0,2,1:T(2,128)(2,1)}, u32[]{:S(2)}, u32[]{:S(2)}) collective-permute-start(bf16[1,2,6,2560]{3,0,2,1:T(2,128)(2,1)} %get-tuple-element.20), channel_id=1, source_target_pairs={{0,6},{2,0},{4,2},{6,4},{1,7},{3,1},{5,3},{7,5},{8,14},{10,8},{12,... | collective-permute-start | bytes 184328 | tf_op jit(solution)/shard_map/ppermute | solution.py:116
  207.3 39.0 %collective-permute-start.5 = (bf16[1,2,6,2560]{3,0,2,1:T(2,128)(2,1)}, bf16[1,2,6,2560]{3,0,2,1:T(2,128)(2,1)}, u32[]{:S(2)}, u32[]{:S(2)}) collective-permute-start(bf16[1,2,6,2560]{3,0,2,1:T(2,128)(2,1)} %get-tuple-element.21), channel_id=1, source_target_pairs={{0,4},{2,6},{4,0},{6,2},{1,5},{3,7},{5,1},{7,3},{8,12},{10,14},{12... | collective-permute-start | bytes 184328 | tf_op jit(solution)/shard_map/ppermute | solution.py:116
  208.8 34.9 %collective-permute-start.4 = (bf16[1,2,6,2560]{3,0,2,1:T(2,128)(2,1)}, bf16[1,2,6,2560]{3,0,2,1:T(2,128)(2,1)}, u32[]{:S(2)}, u32[]{:S(2)}) collective-permute-start(bf16[1,2,6,2560]{3,0,2,1:T(2,128)(2,1)} %get-tuple-element.22), channel_id=1, source_target_pairs={{0,2},{2,4},{4,6},{6,0},{1,3},{3,5},{5,7},{7,1},{8,10},{10,12},{12... | collective-permute-start | bytes 184328 | tf_op jit(solution)/shard_map/ppermute | solution.py:116
  211.1 8.9 %collective-permute-start = (bf16[2,6,10240]{2,0,1:T(2,128)(2,1)S(1)}, bf16[2,6,10240]{2,0,1:T(2,128)(2,1)S(1)}, u32[]{:S(2)}, u32[]{:S(2)}) collective-permute-start(bf16[2,6,10240]{2,0,1:T(2,128)(2,1)S(1)} %add_convert_fusion.5), channel_id=1, source_target_pairs={{8,0},{16,8},{24,16},{9,1},{17,9},{25,17},{10,2},{18,10},{26,18},{... | collective-permute-start | bytes 737288 | tf_op jit(solution)/shard_map/ppermute | solution.py:26
  221.0 21.7 %copy-start.99 = (bf16[2,6,80,128]{3,2,1,0:T(8,128)(2,1)S(1)}, bf16[2,6,80,128]{3,2,1,0:T(8,128)(2,1)}, u32[]{:S(2)}) copy-start(bf16[2,6,80,128]{3,2,1,0:T(8,128)(2,1)} %copy-done.98) | copy-start | bytes 737284
  221.0 21.7 %copy-start.106 = (bf16[2,6,80,128]{3,2,0,1:T(8,128)(2,1)S(1)}, bf16[2,6,80,128]{3,2,0,1:T(8,128)(2,1)}, u32[]{:S(2)}) copy-start(bf16[2,6,80,128]{3,2,0,1:T(8,128)(2,1)} %reshape.1505) | copy-start | bytes 737284
  221.1 22.6 %copy-start.93 = (bf16[4,2,6,2560]{3,0,2,1:T(4,128)(2,1)S(1)}, bf16[4,2,6,2560]{3,0,2,1:T(4,128)(2,1)}, u32[]{:S(2)}) copy-start(bf16[4,2,6,2560]{3,0,2,1:T(4,128)(2,1)} %fusion.426) | copy-start | bytes 737284
  239.1 14.1 %all-to-all-start.2 = ((bf16[4,2,15360]{2,1,0:T(2,128)(2,1)}), bf16[4,2,15360]{2,1,0:T(2,128)(2,1)S(1)}, u32[]{:S(2)}, u32[]{:S(2)}) async-start(bf16[4,2,15360]{2,1,0:T(2,128)(2,1)} %reshape.1827), calls=%async_computation.2 | async-start | bytes 491520 | tf_op jit(solution)/shard_map/all_to_all | solution.py:123
  284.8 10.0 %all-to-all-start.3 = ((bf16[8,6,2560]{2,1,0:T(8,128)(2,1)}), bf16[8,6,2560]{2,1,0:T(8,128)(2,1)}, u32[]{:S(2)}, u32[]{:S(2)}) async-start(bf16[8,6,2560]{2,1,0:T(8,128)(2,1)} %reshape.1821), calls=%async_computation.3 | async-start | bytes 655360 | tf_op jit(solution)/shard_map/all_to_all | solution.py:128
  316.5 26.3 %copy-start.22 = (bf16[128,128,1,1]{1,0,2,3:T(8,128)(2,1)S(1)}, bf16[128,128,1,1]{1,0,2,3:T(8,128)(2,1)}, u32[]{:S(2)}) copy-start(bf16[128,128,1,1]{1,0,2,3:T(8,128)(2,1)} %copy-done.21) | copy-start | bytes 98308
  317.5 26.6 %copy-start.17 = (bf16[128,128,1,1]{1,0,2,3:T(8,128)(2,1)S(1)}, bf16[128,128,1,1]{1,0,2,3:T(8,128)(2,1)}, u32[]{:S(2)}) copy-start(bf16[128,128,1,1]{1,0,2,3:T(8,128)(2,1)} %copy-done.16) | copy-start | bytes 98308
  321.3 23.0 %copy-start.12 = (bf16[128,128,1,1]{1,0,2,3:T(8,128)(2,1)S(1)}, bf16[128,128,1,1]{1,0,2,3:T(8,128)(2,1)}, u32[]{:S(2)}) copy-start(bf16[128,128,1,1]{1,0,2,3:T(8,128)(2,1)} %copy-done.11) | copy-start | bytes 98308
  322.4 67.7 %collective-permute-start.9 = (bf16[1,2,6,2560]{3,0,2,1:T(2,128)(2,1)}, bf16[1,2,6,2560]{3,0,2,1:T(2,128)(2,1)}, u32[]{:S(2)}, u32[]{:S(2)}) collective-permute-start(bf16[1,2,6,2560]{3,0,2,1:T(2,128)(2,1)} %get-tuple-element.17), channel_id=1, source_target_pairs={{0,6},{2,0},{4,2},{6,4},{1,7},{3,1},{5,3},{7,5},{8,14},{10,8},{12,... | collective-permute-start | bytes 184328 | tf_op jit(solution)/shard_map/ppermute | solution.py:116
  323.9 63.5 %collective-permute-start.8 = (bf16[1,2,6,2560]{3,0,2,1:T(2,128)(2,1)}, bf16[1,2,6,2560]{3,0,2,1:T(2,128)(2,1)}, u32[]{:S(2)}, u32[]{:S(2)}) collective-permute-start(bf16[1,2,6,2560]{3,0,2,1:T(2,128)(2,1)} %get-tuple-element.18), channel_id=1, source_target_pairs={{0,4},{2,6},{4,0},{6,2},{1,5},{3,7},{5,1},{7,3},{8,12},{10,14},{12... | collective-permute-start | bytes 184328 | tf_op jit(solution)/shard_map/ppermute | solution.py:116
  325.3 59.3 %collective-permute-start.7 = (bf16[1,2,6,2560]{3,0,2,1:T(2,128)(2,1)}, bf16[1,2,6,2560]{3,0,2,1:T(2,128)(2,1)}, u32[]{:S(2)}, u32[]{:S(2)}) collective-permute-start(bf16[1,2,6,2560]{3,0,2,1:T(2,128)(2,1)} %get-tuple-element.19), channel_id=1, source_target_pairs={{0,2},{2,4},{4,6},{6,0},{1,3},{3,5},{5,7},{7,1},{8,10},{10,12},{12... | collective-permute-start | bytes 184328 | tf_op jit(solution)/shard_map/ppermute | solution.py:116
  351.3 28.9 %copy-start.85 = (bf16[2,6,10240]{2,0,1:T(2,128)(2,1)}, bf16[2,6,10240]{2,0,1:T(2,128)(2,1)S(1)}, u32[]{:S(2)}) copy-start(bf16[2,6,10240]{2,0,1:T(2,128)(2,1)S(1)} %add_convert_fusion.4) | copy-start | bytes 737284
  351.4 10.5 %collective-permute-start.1 = (bf16[2,6,10240]{2,0,1:T(2,128)(2,1)S(1)}, bf16[2,6,10240]{2,0,1:T(2,128)(2,1)S(1)}, u32[]{:S(2)}, u32[]{:S(2)}) collective-permute-start(bf16[2,6,10240]{2,0,1:T(2,128)(2,1)S(1)} %add_convert_fusion.4), channel_id=1, source_target_pairs={{8,0},{16,8},{24,16},{9,1},{17,9},{25,17},{10,2},{18,10},{26,18},{... | collective-permute-start | bytes 737288 | tf_op jit(solution)/shard_map/ppermute | solution.py:26
  362.2 21.8 %copy-start.119 = (f32[128,128]{1,0:T(8,128)S(1)}, f32[128,128]{1,0:T(8,128)}, u32[]{:S(2)}) copy-start(f32[128,128]{1,0:T(8,128)} %convolution_bitcast_fusion.36) | copy-start | bytes 196612
  362.2 21.8 %copy-start.121 = (f32[128,128]{1,0:T(8,128)S(1)}, f32[128,128]{1,0:T(8,128)}, u32[]{:S(2)}) copy-start(f32[128,128]{1,0:T(8,128)} %convolution_bitcast_fusion.27) | copy-start | bytes 196612
  362.2 22.5 %copy-start.95 = (bf16[4,2,6,2560]{3,0,2,1:T(4,128)(2,1)S(1)}, bf16[4,2,6,2560]{3,0,2,1:T(4,128)(2,1)}, u32[]{:S(2)}) copy-start(bf16[4,2,6,2560]{3,0,2,1:T(4,128)(2,1)} %fusion.425) | copy-start | bytes 737284
  380.3 14.0 %all-to-all-start.4 = ((bf16[4,2,15360]{2,1,0:T(2,128)(2,1)}), bf16[4,2,15360]{2,1,0:T(2,128)(2,1)S(1)}, u32[]{:S(2)}, u32[]{:S(2)}) async-start(bf16[4,2,15360]{2,1,0:T(2,128)(2,1)} %reshape.1829), calls=%async_computation.4 | async-start | bytes 491520 | tf_op jit(solution)/shard_map/all_to_all | solution.py:123
  425.8 10.2 %all-to-all-start.5 = ((bf16[8,6,2560]{2,1,0:T(8,128)(2,1)}), bf16[8,6,2560]{2,1,0:T(8,128)(2,1)}, u32[]{:S(2)}, u32[]{:S(2)}) async-start(bf16[8,6,2560]{2,1,0:T(8,128)(2,1)} %reshape.1822), calls=%async_computation.5 | async-start | bytes 655360 | tf_op jit(solution)/shard_map/all_to_all | solution.py:128
  456.0 26.2 %copy-start.23 = (bf16[128,128,1,1]{1,0,2,3:T(8,128)(2,1)S(1)}, bf16[128,128,1,1]{1,0,2,3:T(8,128)(2,1)}, u32[]{:S(2)}) copy-start(bf16[128,128,1,1]{1,0,2,3:T(8,128)(2,1)} %copy-done.21) | copy-start | bytes 98308
  456.9 26.5 %copy-start.18 = (bf16[128,128,1,1]{1,0,2,3:T(8,128)(2,1)S(1)}, bf16[128,128,1,1]{1,0,2,3:T(8,128)(2,1)}, u32[]{:S(2)}) copy-start(bf16[128,128,1,1]{1,0,2,3:T(8,128)(2,1)} %copy-done.16) | copy-start | bytes 98308
  460.8 22.9 %copy-start.13 = (bf16[128,128,1,1]{1,0,2,3:T(8,128)(2,1)S(1)}, bf16[128,128,1,1]{1,0,2,3:T(8,128)(2,1)}, u32[]{:S(2)}) copy-start(bf16[128,128,1,1]{1,0,2,3:T(8,128)(2,1)} %copy-done.11) | copy-start | bytes 98308
  461.8 65.8 %collective-permute-start.12 = (bf16[1,2,6,2560]{3,0,2,1:T(2,128)(2,1)}, bf16[1,2,6,2560]{3,0,2,1:T(2,128)(2,1)}, u32[]{:S(2)}, u32[]{:S(2)}) collective-permute-start(bf16[1,2,6,2560]{3,0,2,1:T(2,128)(2,1)} %get-tuple-element.14), channel_id=1, source_target_pairs={{0,6},{2,0},{4,2},{6,4},{1,7},{3,1},{5,3},{7,5},{8,14},{10,8},{12,... | collective-permute-start | bytes 184328 | tf_op jit(solution)/shard_map/ppermute | solution.py:116
  463.3 61.6 %collective-permute-start.11 = (bf16[1,2,6,2560]{3,0,2,1:T(2,128)(2,1)}, bf16[1,2,6,2560]{3,0,2,1:T(2,128)(2,1)}, u32[]{:S(2)}, u32[]{:S(2)}) collective-permute-start(bf16[1,2,6,2560]{3,0,2,1:T(2,128)(2,1)} %get-tuple-element.15), channel_id=1, source_target_pairs={{0,4},{2,6},{4,0},{6,2},{1,5},{3,7},{5,1},{7,3},{8,12},{10,14},{12... | collective-permute-start | bytes 184328 | tf_op jit(solution)/shard_map/ppermute | solution.py:116
  464.8 57.5 %collective-permute-start.10 = (bf16[1,2,6,2560]{3,0,2,1:T(2,128)(2,1)}, bf16[1,2,6,2560]{3,0,2,1:T(2,128)(2,1)}, u32[]{:S(2)}, u32[]{:S(2)}) collective-permute-start(bf16[1,2,6,2560]{3,0,2,1:T(2,128)(2,1)} %get-tuple-element.16), channel_id=1, source_target_pairs={{0,2},{2,4},{4,6},{6,0},{1,3},{3,5},{5,7},{7,1},{8,10},{10,12},{12... | collective-permute-start | bytes 184328 | tf_op jit(solution)/shard_map/ppermute | solution.py:116
  488.9 28.7 %copy-start.86 = (bf16[2,6,10240]{2,0,1:T(2,128)(2,1)}, bf16[2,6,10240]{2,0,1:T(2,128)(2,1)S(1)}, u32[]{:S(2)}) copy-start(bf16[2,6,10240]{2,0,1:T(2,128)(2,1)S(1)} %add_convert_fusion.3) | copy-start | bytes 737284
  488.9 10.3 %collective-permute-start.2 = (bf16[2,6,10240]{2,0,1:T(2,128)(2,1)S(1)}, bf16[2,6,10240]{2,0,1:T(2,128)(2,1)S(1)}, u32[]{:S(2)}, u32[]{:S(2)}) collective-permute-start(bf16[2,6,10240]{2,0,1:T(2,128)(2,1)S(1)} %add_convert_fusion.3), channel_id=1, source_target_pairs={{8,0},{16,8},{24,16},{9,1},{17,9},{25,17},{10,2},{18,10},{26,18},{... | collective-permute-start | bytes 737288 | tf_op jit(solution)/shard_map/ppermute | solution.py:26
  499.5 21.8 %copy-start.101 = (bf16[2,6,80,128]{3,2,1,0:T(8,128)(2,1)S(1)}, bf16[2,6,80,128]{3,2,1,0:T(8,128)(2,1)}, u32[]{:S(2)}) copy-start(bf16[2,6,80,128]{3,2,1,0:T(8,128)(2,1)} %copy-done.100) | copy-start | bytes 737284
  499.5 21.8 %copy-start.105 = (bf16[2,6,80,128]{3,2,0,1:T(8,128)(2,1)S(1)}, bf16[2,6,80,128]{3,2,0,1:T(8,128)(2,1)}, u32[]{:S(2)}) copy-start(bf16[2,6,80,128]{3,2,0,1:T(8,128)(2,1)} %reshape.1561) | copy-start | bytes 737284
  499.6 22.7 %copy-start.96 = (bf16[4,2,6,2560]{3,0,2,1:T(4,128)(2,1)S(1)}, bf16[4,2,6,2560]{3,0,2,1:T(4,128)(2,1)}, u32[]{:S(2)}) copy-start(bf16[4,2,6,2560]{3,0,2,1:T(4,128)(2,1)} %fusion.424) | copy-start | bytes 737284
  517.6 14.2 %all-to-all-start.6 = ((bf16[4,2,15360]{2,1,0:T(2,128)(2,1)}), bf16[4,2,15360]{2,1,0:T(2,128)(2,1)S(1)}, u32[]{:S(2)}, u32[]{:S(2)}) async-start(bf16[4,2,15360]{2,1,0:T(2,128)(2,1)} %reshape.1831), calls=%async_computation.6 | async-start | bytes 491520 | tf_op jit(solution)/shard_map/all_to_all | solution.py:123
  563.3 10.0 %all-to-all-start.7 = ((bf16[8,6,2560]{2,1,0:T(8,128)(2,1)}), bf16[8,6,2560]{2,1,0:T(8,128)(2,1)}, u32[]{:S(2)}, u32[]{:S(2)}) async-start(bf16[8,6,2560]{2,1,0:T(8,128)(2,1)} %reshape.1823), calls=%async_computation.7 | async-start | bytes 655360 | tf_op jit(solution)/shard_map/all_to_all | solution.py:128
  595.1 26.2 %copy-start.24 = (bf16[128,128,1,1]{1,0,2,3:T(8,128)(2,1)S(1)}, bf16[128,128,1,1]{1,0,2,3:T(8,128)(2,1)}, u32[]{:S(2)}) copy-start(bf16[128,128,1,1]{1,0,2,3:T(8,128)(2,1)} %copy-done.21) | copy-start | bytes 98308
  596.1 26.5 %copy-start.19 = (bf16[128,128,1,1]{1,0,2,3:T(8,128)(2,1)S(1)}, bf16[128,128,1,1]{1,0,2,3:T(8,128)(2,1)}, u32[]{:S(2)}) copy-start(bf16[128,128,1,1]{1,0,2,3:T(8,128)(2,1)} %copy-done.16) | copy-start | bytes 98308
  599.9 22.9 %copy-start.14 = (bf16[128,128,1,1]{1,0,2,3:T(8,128)(2,1)S(1)}, bf16[128,128,1,1]{1,0,2,3:T(8,128)(2,1)}, u32[]{:S(2)}) copy-start(bf16[128,128,1,1]{1,0,2,3:T(8,128)(2,1)} %copy-done.11) | copy-start | bytes 98308
  601.0 68.9 %collective-permute-start.15 = (bf16[1,2,6,2560]{3,0,2,1:T(2,128)(2,1)S(1)}, bf16[1,2,6,2560]{3,0,2,1:T(2,128)(2,1)}, u32[]{:S(2)}, u32[]{:S(2)}) collective-permute-start(bf16[1,2,6,2560]{3,0,2,1:T(2,128)(2,1)S(1)} %get-tuple-element.11), channel_id=1, source_target_pairs={{0,6},{2,0},{4,2},{6,4},{1,7},{3,1},{5,3},{7,5},{8,14},{10,8},{12,... | collective-permute-start | bytes 184328 | tf_op jit(solution)/shard_map/ppermute | solution.py:116
  602.5 64.7 %collective-permute-start.14 = (bf16[1,2,6,2560]{3,0,2,1:T(2,128)(2,1)}, bf16[1,2,6,2560]{3,0,2,1:T(2,128)(2,1)}, u32[]{:S(2)}, u32[]{:S(2)}) collective-permute-start(bf16[1,2,6,2560]{3,0,2,1:T(2,128)(2,1)} %get-tuple-element.12), channel_id=1, source_target_pairs={{0,4},{2,6},{4,0},{6,2},{1,5},{3,7},{5,1},{7,3},{8,12},{10,14},{12... | collective-permute-start | bytes 184328 | tf_op jit(solution)/shard_map/ppermute | solution.py:116
  603.9 60.5 %collective-permute-start.13 = (bf16[1,2,6,2560]{3,0,2,1:T(2,128)(2,1)}, bf16[1,2,6,2560]{3,0,2,1:T(2,128)(2,1)}, u32[]{:S(2)}, u32[]{:S(2)}) collective-permute-start(bf16[1,2,6,2560]{3,0,2,1:T(2,128)(2,1)} %get-tuple-element.13), channel_id=1, source_target_pairs={{0,2},{2,4},{4,6},{6,0},{1,3},{3,5},{5,7},{7,1},{8,10},{10,12},{12... | collective-permute-start | bytes 184328 | tf_op jit(solution)/shard_map/ppermute | solution.py:116
  629.8 30.2 %copy-start.87 = (bf16[2,6,10240]{2,0,1:T(2,128)(2,1)}, bf16[2,6,10240]{2,0,1:T(2,128)(2,1)S(1)}, u32[]{:S(2)}) copy-start(bf16[2,6,10240]{2,0,1:T(2,128)(2,1)S(1)} %add_convert_fusion.2) | copy-start | bytes 737284
  629.8 11.8 %collective-permute-start.3 = (bf16[2,6,10240]{2,0,1:T(2,128)(2,1)S(1)}, bf16[2,6,10240]{2,0,1:T(2,128)(2,1)S(1)}, u32[]{:S(2)}, u32[]{:S(2)}) collective-permute-start(bf16[2,6,10240]{2,0,1:T(2,128)(2,1)S(1)} %add_convert_fusion.2), channel_id=1, source_target_pairs={{8,0},{16,8},{24,16},{9,1},{17,9},{25,17},{10,2},{18,10},{26,18},{... | collective-permute-start | bytes 737288 | tf_op jit(solution)/shard_map/ppermute | solution.py:26
  641.9 21.8 %copy-start.118 = (f32[128,128]{1,0:T(8,128)S(1)}, f32[128,128]{1,0:T(8,128)}, u32[]{:S(2)}) copy-start(f32[128,128]{1,0:T(8,128)} %convolution_bitcast_fusion.18) | copy-start | bytes 196612
  641.9 21.8 %copy-start.120 = (f32[128,128]{1,0:T(8,128)S(1)}, f32[128,128]{1,0:T(8,128)}, u32[]{:S(2)}) copy-start(f32[128,128]{1,0:T(8,128)} %convolution_bitcast_fusion.9) | copy-start | bytes 196612
  641.9 22.5 %copy-start.94 = (bf16[4,2,6,2560]{3,0,2,1:T(4,128)(2,1)S(1)}, bf16[4,2,6,2560]{3,0,2,1:T(4,128)(2,1)}, u32[]{:S(2)}) copy-start(bf16[4,2,6,2560]{3,0,2,1:T(4,128)(2,1)} %fusion.423) | copy-start | bytes 737284
  660.0 14.0 %all-to-all-start.8 = ((bf16[4,2,15360]{2,1,0:T(2,128)(2,1)}), bf16[4,2,15360]{2,1,0:T(2,128)(2,1)S(1)}, u32[]{:S(2)}, u32[]{:S(2)}) async-start(bf16[4,2,15360]{2,1,0:T(2,128)(2,1)} %reshape.1833), calls=%async_computation.8 | async-start | bytes 491520 | tf_op jit(solution)/shard_map/all_to_all | solution.py:123
  700.6 9.9 %all-to-all-start.9 = ((bf16[8,6,2560]{2,1,0:T(8,128)(2,1)}), bf16[8,6,2560]{2,1,0:T(8,128)(2,1)S(1)}, u32[]{:S(2)}, u32[]{:S(2)}) async-start(bf16[8,6,2560]{2,1,0:T(8,128)(2,1)} %reshape.1824), calls=%async_computation.9 | async-start | bytes 655360 | tf_op jit(solution)/shard_map/all_to_all | solution.py:128
  705.0 100.0 %all-reduce.17.cloned.1.call-start = ((), (), s32[]{:S(2)}) async-start(), calls=%async_computation.10 | async-start | bytes 589824 | tf_op jit(solution)/shard_map/psum | solution.py:162
  739.4 21.3 %copy-start.20 = (bf16[128,128,1,1]{1,0,2,3:T(8,128)(2,1)S(1)}, bf16[128,128,1,1]{1,0,2,3:T(8,128)(2,1)}, u32[]{:S(2)}) copy-start(bf16[128,128,1,1]{1,0,2,3:T(8,128)(2,1)} %copy-done.16) | copy-start | bytes 98308
  741.9 34.2 %collective-permute-start.18 = (bf16[1,2,6,2560]{3,0,2,1:T(2,128)(2,1)}, bf16[1,2,6,2560]{3,0,2,1:T(2,128)(2,1)}, u32[]{:S(2)}, u32[]{:S(2)}) collective-permute-start(bf16[1,2,6,2560]{3,0,2,1:T(2,128)(2,1)} %get-tuple-element.8), channel_id=1, source_target_pairs={{0,6},{2,0},{4,2},{6,4},{1,7},{3,1},{5,3},{7,5},{8,14},{10,8},{12,... | collective-permute-start | bytes 184328 | tf_op jit(solution)/shard_map/ppermute | solution.py:116
  743.3 30.0 %collective-permute-start.17 = (bf16[1,2,6,2560]{3,0,2,1:T(2,128)(2,1)}, bf16[1,2,6,2560]{3,0,2,1:T(2,128)(2,1)}, u32[]{:S(2)}, u32[]{:S(2)}) collective-permute-start(bf16[1,2,6,2560]{3,0,2,1:T(2,128)(2,1)} %get-tuple-element.9), channel_id=1, source_target_pairs={{0,4},{2,6},{4,0},{6,2},{1,5},{3,7},{5,1},{7,3},{8,12},{10,14},{12... | collective-permute-start | bytes 184328 | tf_op jit(solution)/shard_map/ppermute | solution.py:116
  744.8 25.8 %collective-permute-start.16 = (bf16[1,2,6,2560]{3,0,2,1:T(2,128)(2,1)}, bf16[1,2,6,2560]{3,0,2,1:T(2,128)(2,1)}, u32[]{:S(2)}, u32[]{:S(2)}) collective-permute-start(bf16[1,2,6,2560]{3,0,2,1:T(2,128)(2,1)} %get-tuple-element.10), channel_id=1, source_target_pairs={{0,2},{2,4},{4,6},{6,0},{1,3},{3,5},{5,7},{7,1},{8,10},{10,12},{12... | collective-permute-start | bytes 184328 | tf_op jit(solution)/shard_map/ppermute | solution.py:116
  (96 other events, 963.1 us)
Sparse Core Ops, SparseCore 0:
  739.5 53.5 all-reduce.16
